TPU v7x, 128 devices: a whole 4x4x4 slice. The times are simulated.
128 devices in a mesh: occ: 4 (over y_hi, core), aux: 32 (over x, z, y_lo).
Axes of the slice: x: 4, y: 4 (y_hi: 2, y_lo: 2; y = y_hi * 2 + y_lo), z: 4, core: 2. Of those that a mesh axis runs over, the one named last changes fastest.
Arguments:
- three_index: bfloat16 [12000, 6, 1920], P('aux'), may hold values from -0.47851562 to 0.47851562
- occ_energy: float32 [6], replicated, may hold values from -1.5 to -0.3
- vir_energy: float32 [1920], replicated, may hold values from 0.25 to 2.95
- batch_table: int32 [6], replicated, may hold values from 0 to 5, each once
- orbital_order: int32 [6], replicated, may hold values from 0 to 5, each once
- occ_pair_int: bfloat16 [2, 2, 12000], P(None, None, 'aux'), may hold values from -0.03881836 to 0.03881836
- half_ao: bfloat16 [2, 12000, 4000], P(None, 'aux'), may hold values from -9.536743e-06 to 9.536743e-06
- vir_coeff: bfloat16 [4000, 1920], P('aux', 'occ'), may hold values from -0.09375 to 0.09375
Outputs:
- gamma: bfloat16 [12000, 2, 1920], P('aux', None, 'occ')
- orbital_gradient: float32 [2, 1920], P(None, ('occ', 'aux'))
Inputs may be any that keep to these rules, and one draw needn't show every extreme that they name: `batch_table`: a permutation of 0 to 5; its first 4 entries are the partner orbitals of the window. `orbital_order`: a permutation of 0 to 5; its first 2 entries are the orbitals whose amplitudes are formed.
All inputs are finite; a program needn't handle non-finite values.
Results may differ from a plain program's by a relative error of at most 0.019.
Values may be sent and summed in bfloat16 or wider, within the bound.
No kernel may reach another device: no remote copies, remote signals or barrier semaphores. Data moves between devices by JAX's collectives and lax.ppermute only.
A program may use at most 128 MiB of HBM per device.

v0:
```python
import functools

import jax
import jax.numpy as jnp
from jax import lax
from jax.sharding import Mesh
from jax.sharding import PartitionSpec as P

NI = 2
NPART_DEV = 1
AUX = ("aux_0", "aux_1", "aux_2")
OCC = ("occ_0", "occ_1")
OCC_AUX = ("occ_0", "occ_1", "aux_0", "aux_1", "aux_2")


def own_rows(terms, axes):
    so_far = terms.astype(jnp.bfloat16)
    for axis in axes:
        so_far = lax.psum_scatter(so_far, axis, scatter_dimension=0, tiled=True)
    return so_far.astype(jnp.float32)


def one_axis_at_a_time(shard, axes):
    return functools.reduce(lax.psum, axes, shard)


def in_blocks(shard, dim, count):
    before, after = (shard.shape[:dim], shard.shape[dim + 1 :])
    return jnp.moveaxis(shard.reshape(*before, count, -1, *after), dim, 0)


def sent_and_summed(shard, axis, dim):
    count = lax.axis_size(axis)
    pieces = lax.all_to_all(in_blocks(shard, dim, count), axis, 0, 0, tiled=True)
    return jnp.sum(pieces, axis=0)


def local(
    three_index,
    occ_energy,
    vir_energy,
    batch_table,
    orbital_order,
    occ_pair_int,
    half_ao,
    vir_coeff,
):
    aux_width = lax.axis_size(AUX)
    nvirt = three_index.shape[2]
    row_share = nvirt // aux_width
    occ_place = lax.axis_index(OCC)
    aux_place = lax.axis_index(AUX)
    own_orbits = orbital_order[:NI]
    my_partners = lax.dynamic_slice_in_dim(batch_table, occ_place * NPART_DEV, NPART_DEV)
    left_block = jnp.take(three_index, own_orbits, axis=1)
    right_block = jnp.take(three_index, my_partners, axis=1)
    left_energy = jnp.take(occ_energy, own_orbits)
    right_energy = jnp.take(occ_energy, my_partners)
    pair_block = jnp.einsum(
        "qsa,qkb->askb", left_block, right_block, preferred_element_type=jnp.float32
    )
    pair_rows = own_rows(
        pair_block.reshape(row_share * lax.axis_size(AUX), NI * NPART_DEV * nvirt), AUX
    )
    row_count = pair_rows.shape[0]
    shaped = pair_rows.reshape(row_count, NI, NPART_DEV, nvirt)
    row_energy = lax.dynamic_slice_in_dim(vir_energy, aux_place * row_share, row_count)
    denominator = (
        row_energy[:, None, None, None]
        + vir_energy[None, None, None, :]
        - left_energy[None, :, None, None]
        - right_energy[None, None, :, None]
    )
    amps_rows = (-shaped / denominator).astype(jnp.bfloat16)
    gamma_part = jnp.einsum(
        "askb,qkb->qsa",
        lax.all_gather(amps_rows, AUX, axis=0, tiled=True),
        right_block,
        preferred_element_type=jnp.float32,
    )
    gamma_out = lax.psum_scatter(
        gamma_part.astype(jnp.bfloat16), OCC, scatter_dimension=2, tiled=True
    )
    density_part = -jnp.einsum(
        "askb,atkb->st", amps_rows, amps_rows, preferred_element_type=jnp.float32
    )
    density = one_axis_at_a_time(density_part, OCC_AUX)
    pair_int = occ_pair_int.astype(jnp.float32)
    coulomb = jnp.einsum("stq,st->q", pair_int, density, precision=lax.Precision.HIGHEST)
    exchange = jnp.einsum("suq,tu->stq", pair_int, density, precision=lax.Precision.HIGHEST)
    identity = jnp.eye(NI, dtype=jnp.float32)
    coefficient = (2.0 * identity[:, :, None] * coulomb[None, None, :] - exchange).astype(
        jnp.bfloat16
    )
    aux_rows = half_ao.shape[1]
    fock_part = jnp.dot(
        coefficient.reshape(NI, NI * aux_rows),
        half_ao.reshape(NI * aux_rows, half_ao.shape[2]),
        preferred_element_type=jnp.float32,
    )
    occ_side = -jnp.einsum(
        "usq,qua->sa", occ_pair_int, gamma_out, preferred_element_type=jnp.float32
    )
    fock_tile = sent_and_summed(fock_part, AUX, 1)
    vir_side = jnp.dot(fock_tile, vir_coeff.astype(jnp.float32), precision=lax.Precision.HIGHEST)
    gradient = sent_and_summed(occ_side + vir_side, AUX, 1)
    return (gamma_out, gradient)


def solution(mesh):
    torus = Mesh(mesh.devices.reshape(2, 2, 4, 4, 2), ("occ_0", "occ_1", "aux_0", "aux_1", "aux_2"))
    return jax.shard_map(
        local,
        mesh=torus,
        in_specs=(
            P(AUX, None, None),
            P(),
            P(),
            P(),
            P(),
            P(None, None, AUX),
            P(None, AUX, None),
            P(AUX, OCC),
        ),
        out_specs=(P(AUX, None, OCC), P(None, OCC_AUX)),
        check_vma=False,
    )
```

profile of v0, /device:TPU:0, one launch (start us, length us, event | category | flops | bytes accessed | tf_op | source)
XLA Modules:
  0.0 715.4 jit_solution(11130920844778028338)
XLA Ops:
  7.2 1.2 dynamic_slice.6
  10.4 0.7 compare_and_fusion
  11.1 4.5 gather_fusion
  15.6 12.4 %convolution_convert_fusion = bf16[1920,2,1920]{2,0,1:T(8,128)(2,1)} fusion(bf16[2,375,1920]{2,1,0:T(8,128)(2,1)S(1)} %gather_fusion, pred[2]{0:T(512)(128)(4,1)S(1)} %get-tuple-element.30, bf16[375,6,1920]{2,0,1:T(8,128)(2,1)} %param.8, s32[]{:T(128)} %bitcast.1, pred[]{:T(512)} %bitcast), kind=kOutput, calls=%fused_computation.5 | convolution fusion | flops 5539132928 | bytes 19070466 | tf_op jit(solution)/shard_map/qsa,qkb->askb/dot_general | solution.py:59
  27.9 20.1 %copy.19 = bf16[1920,3840]{1,0:T(8,128)(2,1)} copy(bf16[1920,3840]{0,1:T(8,128)(2,1)} %bitcast.75) | data formatting | bytes 29491200 | tf_op jit(solution)/shard_map/convert_element_type | solution.py:17
  48.2 134.6 %reduce-scatter.5.cloned.1.call-done = bf16[480,3840]{1,0:T(8,128)(2,1)} async-done(((bf16[1920,3840]{1,0:T(8,128)(2,1)}), bf16[480,3840]{1,0:T(8,128)(2,1)}) %reduce-scatter.5.cloned.1.call-update) | async-done | bytes 3686416 | tf_op jit(solution)/shard_map/reduce_scatter | solution.py:19
  182.8 0.6 gather_fusion.1
  183.6 44.2 %reduce-scatter.7.cloned.1.call-done = bf16[120,3840]{1,0:T(8,128)(2,1)} async-done(((bf16[480,3840]{1,0:T(8,128)(2,1)}), bf16[120,3840]{1,0:T(8,128)(2,1)}) %reduce-scatter.7.cloned.1.call-update) | async-done | bytes 921616 | tf_op jit(solution)/shard_map/reduce_scatter | solution.py:19
  227.9 16.9 %fusion = bf16[64,3840]{1,0:T(8,128)(2,1)S(1)} fusion(bf16[120,3840]{1,0:T(8,128)(2,1)} %reduce-scatter.7.cloned.1.call-done), kind=kCustom, calls=%all-reduce-scatter | all-reduce-scatter fusion | flops 491521 | bytes 1413632
  244.8 2.4 collective-permute-start
  248.6 0.7 dynamic-slice.13
  250.7 0.7 concatenate.2
  251.4 1.1 divide_convert_fusion
  253.0 1.5 fusion.29
  254.7 317.7 %all-gather.2.cloned.1.call-done = bf16[1920,2,1,1920]{3,1,2,0:T(2,128)(2,1)} async-done(((bf16[60,2,1,1920]{3,1,2,0:T(2,128)(2,1)}), bf16[1920,2,1,1920]{3,1,2,0:T(2,128)(2,1)}) %all-gather.2.cloned.1.call-update) | async-done | bytes 14745616 | tf_op jit(solution)/shard_map/all_gather | solution.py:77
  572.4 13.1 %fusion.9 = bf16[375,2,1920]{2,0,1:T(8,128)(2,1)S(1)} fusion(bf16[1920,2,1,1920]{3,1,2,0:T(2,128)(2,1)} %all-gather.2.cloned.1.call-done, bf16[375,6,1920]{2,0,1:T(8,128)(2,1)} %param.8, s32[]{:T(128)} %bitcast.1, pred[]{:T(512)} %bitcast), kind=kOutput, calls=%fused_computation.9 | convolution fusion | flops 5531759616 | bytes 19070464 | tf_op jit(solution)/shard_map/askb,qkb->qsa/dot_general | solution.py:75
  585.6 7.0 copy.22
  592.8 1.6 fusion.25
  594.3 6.4 psum.35
  600.8 2.4 psum.36
  603.2 10.0 %copy.24 = bf16[2,375,4000]{2,1,0:T(8,128)(2,1)} copy(bf16[2,375,4000]{2,0,1:T(2,128)(2,1)} %param.14) | data formatting | bytes 12000000 | tf_op args[6]
  613.2 10.7 %psum.37 = f32[2,2]{1,0:T(2,128)S(1)} all-reduce(f32[2,2]{1,0:T(2,128)S(1)} %psum.36), channel_id=1, replica_groups=mesh['occ_0'=2,'occ_1'=2,'aux_0'=4,'aux_1'=4,'aux_2'=2] {'aux_0'}, use_global_device_ids=true, to_apply=%region_6.7 | all-reduce | flops 4 | bytes 32 | tf_op jit(solution)/shard_map/psum | solution.py:24
  623.9 8.1 %reshape.144 = bf16[750,4000]{1,0:T(8,128)(2,1)} reshape(bf16[2,375,4000]{2,1,0:T(8,128)(2,1)} %copy.24) | data formatting | bytes 12000000 | tf_op jit(solution)/shard_map/reshape | solution.py:98
  632.0 10.6 %psum.38 = f32[2,2]{1,0:T(2,128)S(1)} all-reduce(f32[2,2]{1,0:T(2,128)S(1)} %psum.37), channel_id=1, replica_groups=mesh['occ_0'=2,'occ_1'=2,'aux_0'=4,'aux_1'=4,'aux_2'=2] {'aux_1'}, use_global_device_ids=true, to_apply=%region_7.8 | all-reduce | flops 4 | bytes 32 | tf_op jit(solution)/shard_map/psum | solution.py:24
  642.7 28.6 %dot_general.35 = bf16[32,125,750]{1,0,2:T(8,128)(2,1)} reshape(bf16[4000,750]{0,1:T(8,128)(2,1)} %bitcast.74) | data formatting | bytes 12000000 | tf_op jit(solution)/shard_map/dot_general | solution.py:96
  671.3 5.0 psum.39
  676.8 5.1 fusion.18
  681.8 3.9 all-to-all-start
  686.9 7.0 all-to-all-done
  694.0 1.6 constant_dynamic-slice_fusion
  696.5 11.7 %all_to_all.10 = f32[32,2,15]{2,1,0:T(2,128)S(1)} all-to-all(f32[32,2,15]{2,1,0:T(2,128)S(1)} %copy.26), channel_id=1, replica_groups=mesh['occ_0'=2,'occ_1'=2,'aux_0'=4,'aux_1'=4,'aux_2'=2] {'aux_0','aux_1'..., dimensions={0} | all-to-all | bytes 7680 | tf_op jit(solution)/shard_map/all_to_all | solution.py:34
  708.2 0.6 reduce_sum.19
  (50 shorter events, 4.7 us)
Async XLA Ops:
  7.2 688.9 %copy-start = (bf16[125,480]{0,1:T(8,128)(2,1)S(1)}, bf16[125,480]{0,1:T(8,128)(2,1)}, u32[]{:S(2)}) copy-start(bf16[125,480]{0,1:T(8,128)(2,1)} %param.15) | copy-start | bytes 360004
  7.2 175.5 %reduce-scatter.5.cloned.1.call-start = ((), (), s32[]{:S(2)}) async-start(), calls=%async_computation.4 | async-start | bytes 18432000 | tf_op jit(solution)/shard_map/reduce_scatter | solution.py:19
  48.1 134.7 %copy-start.1 = (f32[6]{0:T(128)S(1)}, f32[6]{0:T(128)}, u32[]{:S(2)}) copy-start(f32[6]{0:T(128)} %param.9) | copy-start | bytes 76
  48.1 135.4 %copy-start.4 = (f32[1920]{0:T(1024)S(1)}, f32[1920]{0:T(1024)}, u32[]{:S(2)}) copy-start(f32[1920]{0:T(1024)} %param.10) | copy-start | bytes 23044
  48.1 179.8 %reduce-scatter.7.cloned.1.call-start = ((), (), s32[]{:S(2)}) async-start(), calls=%async_computation.5 | async-start | bytes 4608000 | tf_op jit(solution)/shard_map/reduce_scatter | solution.py:19
  182.7 65.9 %copy-start.6 = (u32[128]{0:T(128)S(1)}, u32[128]{0:T(128)}, u32[]{:S(2)}) copy-start(u32[128]{0:T(128)} %constant.137) | copy-start | bytes 1540
  182.7 389.7 %all-gather.2.cloned.1.call-start = ((), (), s32[]{:S(2)}) async-start(), calls=%async_computation.6 | async-start | bytes 15206400 | tf_op jit(solution)/shard_map/all_gather | solution.py:77
  244.8 5.9 collective-permute-start
  254.5 439.5 %all-reduce.5.cloned.1.call-start = ((), (), s32[]{:S(2)}) async-start(), calls=%async_computation.7 | async-start | bytes 5898240
  585.6 7.0 copy-start.3
  642.7 33.6 %copy-start.5 = (bf16[2,2,375]{2,1,0:T(2,128)(2,1)S(1)}, bf16[2,2,375]{2,1,0:T(2,128)(2,1)}, u32[]{:S(2)}) copy-start(bf16[2,2,375]{2,1,0:T(2,128)(2,1)} %param.13) | copy-start | bytes 9004
  671.3 14.4 %copy-start.7 = (u32[128]{0:T(128)S(1)}, u32[128]{0:T(128)}, u32[]{:S(2)}) copy-start(u32[128]{0:T(128)} %constant.141) | copy-start | bytes 1540
  681.8 12.1 %all-to-all-start = ((f32[32,2,125]{2,1,0:T(2,128)}), f32[32,2,125]{2,1,0:T(2,128)S(1)}, u32[]{:S(2)}, u32[]{:S(2)}) async-start(f32[32,2,125]{2,1,0:T(2,128)} %fusion.18), calls=%async_computation.2 | async-start | bytes 65536 | tf_op jit(solution)/shard_map/all_to_all | solution.py:34
  695.7 13.1 %copy-start.2 = (bf16[375,2,480]{0,2,1:T(8,128)(2,1)}, bf16[375,2,480]{0,2,1:T(8,128)(2,1)S(1)}, u32[]{:S(2)}) copy-start(bf16[375,2,480]{0,2,1:T(8,128)(2,1)S(1)} %copy.27) | copy-start | bytes 2160004
Sparse Core Ops, SparseCore 0:
  48.2 134.4 reduce-scatter.4
  185.1 42.6 reduce-scatter.6
  254.6 317.7 all-gather.1
  592.7 75.0 all-reduce.4
where the time goes:
time: 717 us; the launch traced here: 715 us
  waiting for transfers between devices  504 us (70%)
  local copies, waits for them, and re-layouts  86.4 us (12%)
  blocking collectives  63.8 us (9%)
  matrix products  33 us (5%)
  between operations  18 us (3%)
    all_gather x1, waiting for transfers between devices, local(): lax.all_gather(amps_rows, AUX, axis=0, tiled=True)  318 us
    reduce_scatter x2, waiting for transfers between devices, own_rows(): so_far = lax.psum_scatter(so_far, axis, scatter_dimension=0, tiled=True)  179 us
    psum x5, blocking collectives, one_axis_at_a_time(): return functools.reduce(lax.psum, axes, shard)  35.2 us
    dot_general x1, local copies, waits for them, and re-layouts, local(): jnp.dot(coefficient.reshape(NI, NI * aux_rows), half_ao.reshape(NI * aux_...  28.6 us
    convert_element_type x1, local copies, waits for them, and re-layouts, own_rows(): so_far = terms.astype(jnp.bfloat16)  20.1 us
    unnamed x1, blocking collectives  16.9 us
  transfers between devices with their start and end apart: 6, of which 4 were waited for; matrix products, arithmetic and copies ran while one was open for 8% of the time, Pallas kernels for 0%

commit v1 on v0

v1 whole, which is shorter than its diff:
```python
import jax
import jax.numpy as jnp
from jax import lax
from jax.sharding import Mesh
from jax.sharding import PartitionSpec as P

NI = 2
KH = 2
ROWS = 30
PAD = 32
AUX = ("x", "z", "yl")
OCC_AUX = ("yh", "core", "x", "z", "yl")
F32 = jnp.float32
BF16 = jnp.bfloat16


def ring(n, d):
    return [(i, (i + d) % n) for i in range(n)]


def up(v, axis):
    return lax.ppermute(v, axis, ring(4, 1))


def down(v, axis):
    return lax.ppermute(v, axis, ring(4, -1))


def dot(a, b, dims):
    return lax.dot_general(a, b, (dims, ((), ())), preferred_element_type=F32)


def ring_sum(v, axis):
    lo2, hi2 = v[2]
    got_up = up(lo2.astype(BF16), axis)
    got_down = down(hi2.astype(BF16), axis)
    one = jnp.concatenate([v[1][0] + got_up.astype(F32), v[1][1]]).astype(BF16)
    three = jnp.concatenate([v[3][0], v[3][1] + got_down.astype(F32)]).astype(BF16)
    from_below = up(one, axis)
    from_above = down(three, axis)
    own = jnp.concatenate([v[0][0], v[0][1]])
    return own + from_below.astype(F32) + from_above.astype(F32)


def ring_gather(v, axis):
    below = up(v, axis)
    above = down(v, axis)
    half = v.shape[0] // 2
    lo = up(below[:half], axis)
    hi = down(above[half:], axis)
    return [v, above, jnp.concatenate([lo, hi]), below]


def local(
    three_index,
    occ_energy,
    vir_energy,
    batch_table,
    orbital_order,
    occ_pair_int,
    half_ao,
    vir_coeff,
):
    nq, _, nvirt = three_index.shape
    yh, core, x, z, yl = (lax.axis_index(a) for a in OCC_AUX)
    own_a = (yh * 2 + core) * (nvirt // 4)
    by_orbital = jnp.transpose(three_index, (1, 0, 2))

    def orbital(i):
        return lax.dynamic_index_in_dim(by_orbital, i, 0, keepdims=False)

    def partner_orbital(half, k):
        return lax.dynamic_index_in_dim(batch_table, half * KH + k, 0, keepdims=False)

    pairs = []
    for h in range(2):
        for c in range(2):
            for t in range(2):
                src = h * 4 + c * 2 + t
                dst = (h if c == 0 else 1 - h) * 4 + c * 2 + (1 - t)
                pairs.append((src, dst))
    swap = lambda v: lax.ppermute(v, ("yh", "core", "yl"), pairs)
    right_sent = orbital(partner_orbital(1 - yl, core))
    right_first = swap(right_sent)
    right_second = lax.ppermute(right_first, "core", [(0, 1), (1, 0)])

    place = lax.broadcasted_iota(jnp.int32, (16 * PAD, 1), 0)
    dx, dz, r = place // (4 * PAD), (place // PAD) % 4, place % PAD
    chunk = ((x + dx) % 4) * 4 + (z + dz) % 4
    virt = jnp.where(r < ROWS, chunk * ROWS + r, -nvirt)

    def left_rows(first):
        hot = (lax.broadcasted_iota(jnp.int32, (1, nvirt), 1) == virt + first).astype(BF16)
        both = [
            dot(hot, orbital(orbital_order[s]), ((1,), (1,))).astype(BF16).reshape(16, 1, PAD, nq)
            for s in range(NI)
        ]
        return jnp.concatenate(both, axis=1).reshape(16 * NI * PAD, nq)

    target_yh = jnp.where(core == 0, yh, 1 - yh)
    left_own = left_rows(own_a)
    left_sent = left_rows((target_yh * 2 + core) * (nvirt // 4))
    left_other = swap(left_sent)

    right_own = [orbital(partner_orbital(yl, k)) for k in range(KH)]
    right_other = [
        jnp.where(core == 0, right_first, right_second),
        jnp.where(core == 0, right_second, right_first),
    ]

    pair_flat = occ_pair_int.reshape(NI * NI, nq)
    g = [dot(pair_flat, half_ao[t], ((1,), (0,))) for t in range(NI)]
    cell = lambda u, v, t: g[t][u * NI + v]
    fock_terms = []
    for s in range(NI):
        fock_terms.append(2.0 * cell(0, 0, s) - cell(s, 0, 0))
        fock_terms.append(2.0 * (cell(0, 1, s) + cell(1, 0, s)) - cell(s, 1, 0) - cell(s, 0, 1))
        fock_terms.append(2.0 * cell(1, 1, s) - cell(s, 1, 1))
    fock_terms = jnp.stack(fock_terms)
    n_aux = lax.axis_size(AUX)
    tile = half_ao.shape[2] // n_aux
    fock_tile = lax.psum_scatter(
        fock_terms.reshape(6, n_aux, tile).transpose(1, 0, 2), AUX, scatter_dimension=0, tiled=False
    )
    vir_part = jnp.dot(fock_tile, vir_coeff.astype(F32), precision=lax.Precision.HIGHEST)
    share = vir_part.shape[1] // n_aux
    vir_own = lax.psum_scatter(
        vir_part.reshape(6, n_aux, share).transpose(1, 0, 2), AUX, scatter_dimension=0, tiled=False
    )

    pair_other = lax.ppermute(pair_flat, "yl", [(0, 1), (1, 0)])
    z_part = jnp.stack(
        [
            dot(pair_flat, right_own[k], ((1,), (0,))) + dot(pair_other, right_other[k], ((1,), (0,)))
            for k in range(KH)
        ]
    )
    z_sum = lax.psum(z_part, ("x", "z"))

    def by_block(left, swapped):
        blocks = left.reshape(4, 4, NI * PAD, nq)
        blocks = blocks.transpose(1, 0, 2, 3) if swapped else blocks
        return blocks.reshape(4, 2, 2 * NI * PAD, nq)

    summed = []
    for k, (first, second) in enumerate((("x", "z"), ("z", "x"))):
        lo_, oo_ = by_block(left_own, k == 1), by_block(left_other, k == 1)
        v = {}
        for d in (2, 1, 3, 0):
            v[d] = [
                dot(lo_[d, h], right_own[k], ((1,), (0,))) + dot(oo_[d, h], right_other[k], ((1,), (0,)))
                for h in range(2)
            ]
        u = ring_sum(v, first).reshape(4, 2, PAD, nvirt)
        w = ring_sum([[u[d, 0], u[d, 1]] for d in range(4)], second)
        summed.append(w.reshape(NI, PAD, nvirt))

    own_chunk = x * 4 + z
    padded = jnp.concatenate([vir_energy, vir_energy[:2]])
    row_energy = lax.dynamic_slice_in_dim(padded, own_a + own_chunk * ROWS, PAD)
    left_energy = jnp.stack([occ_energy[orbital_order[s]] for s in range(NI)])
    amps = []
    for k in range(KH):
        e_k = lax.dynamic_index_in_dim(occ_energy, partner_orbital(yl, k), 0, keepdims=False)
        denominator = (
            row_energy[None, :, None] + vir_energy[None, None, :] - left_energy[:, None, None] - e_k
        )
        amps.append((-summed[k] / denominator).astype(BF16))

    wide = [a.astype(F32) for a in amps]
    entries = [
        -sum(jnp.sum(w[s] * w[t]) for w in wide) for s, t in ((0, 0), (0, 1), (1, 1))
    ]
    density = lax.psum(jnp.stack(entries), OCC_AUX)
    occ_rows = []
    for s in range(NI):
        row = jnp.zeros((PAD,), F32)
        for k in range(KH):
            for u in range(NI):
                row = row - jnp.sum(wide[k][u] * z_sum[k, u * NI + s][None, :], axis=1)
        occ_rows.append(row)
    occ_rows = jnp.stack(occ_rows)
    mine = lax.dynamic_slice_in_dim(occ_rows, yl * share, share, axis=1)
    theirs = lax.dynamic_slice_in_dim(occ_rows, (1 - yl) * share, share, axis=1)
    occ_side = mine + lax.ppermute(theirs, "yl", [(0, 1), (1, 0)])

    gammas = []
    for k, (first, second) in enumerate((("z", "x"), ("x", "z"))):
        own = jnp.concatenate(ring_gather(amps[k].reshape(NI * PAD, nvirt), first))
        blocks = ring_gather(own, second)
        parts = [
            [dot(b, right[k], ((1,), (1,))) for b in blocks] for right in (right_other, right_own)
        ]
        both = [jnp.concatenate(p).reshape(4, 4, NI * PAD, nq) for p in parts]
        if k == 1:
            both = [b.transpose(1, 0, 2, 3) for b in both]
        gammas.append(both)
    gamma_sent = (gammas[0][0] + gammas[1][0]).astype(BF16)
    gamma_got = lax.ppermute(gamma_sent, "yl", [(0, 1), (1, 0)])
    gamma_rows = (gammas[0][1] + gammas[1][1] + gamma_got.astype(F32)).astype(BF16)
    gamma_rows = gamma_rows.reshape(16, NI, PAD, nq)
    target = lax.broadcasted_iota(jnp.int32, (nvirt // 4, 1), 0)
    back = (target == virt.reshape(1, 16 * PAD)).astype(BF16)
    gamma_out = jnp.stack(
        [
            dot(back, gamma_rows[:, s].reshape(16 * PAD, nq), ((1,), (0,))).astype(BF16)
            for s in range(NI)
        ]
    )
    gamma_out = jnp.transpose(gamma_out, (2, 0, 1))

    weights = vir_own.reshape(NI, 3, share)
    gradient = occ_side + jnp.sum(weights * density[None, :, None], axis=1)
    return (gamma_out, gradient)


def solution(mesh):
    torus = Mesh(mesh.devices.reshape(2, 2, 4, 4, 2), OCC_AUX)
    occ = ("yh", "core")
    return jax.shard_map(
        local,
        mesh=torus,
        in_specs=(
            P(AUX, None, None),
            P(),
            P(),
            P(),
            P(),
            P(None, None, AUX),
            P(None, AUX, None),
            P(AUX, occ),
        ),
        out_specs=(P(AUX, None, occ), P(None, OCC_AUX)),
        check_vma=False,
    )
```

time: 717 us -> 845 us (1.18)
  waiting for transfers between devices: 504 us -> 249 us
  blocking collectives: 63.8 us -> 291 us
  matrix products: 33 us -> 107 us
  starting transfers between devices: 6.62 us -> 57.4 us
  other arithmetic: 3.96 us -> 21.1 us
  between operations: 18 us -> 28.4 us
    all_gather x1 -> x0, waiting for transfers between devices: 318 us -> none  [local(): lax.all_gather(amps_rows, AUX, axis=0, tiled=True)]
    unnamed x6 -> x2, waiting for transfers between devices: 0.08 us -> 221 us
    reduce_scatter x2 -> x0, waiting for transfers between devices: 179 us -> none  [own_rows(): so_far = lax.psum_scatter(so_far, axis, scatter_dimension=0, tiled=True)]
    unnamed x1, blocking collectives: 16.9 us -> 155 us
    psum x5 -> x2, blocking collectives: 35.2 us -> 136 us  [the longest x1 70.3 us: local(): z_sum = lax.psum(z_part, ('x', 'z'))]
    dot_general x8 -> x61, matrix products: 33 us -> 107 us  [the longest x60 105 us: dot(): return lax.dot_general(a, b, (dims, ((), ())), preferred_element_type=F32)]
    ppermute x0 -> x38, starting transfers between devices: none -> 57.4 us  [the longest x16 45.5 us: down(): return lax.ppermute(v, axis, ring(4, -1))]
    unnamed x25 -> x108, local copies, waits for them, and re-layouts: 14.2 us -> 43.6 us
  transfers between devices with their start and end apart: 6 -> 39, of which waited for: 4 -> 10; matrix products, arithmetic and copies ran while one was open for 8% -> 22% of each run, Pallas kernels for 0% -> 0%
where the time goes in v1:
time: 845 us; the launch traced here: 839 us
  blocking collectives  291 us (34%)
  waiting for transfers between devices  249 us (29%)
  matrix products  107 us (13%)
  local copies, waits for them, and re-layouts  85.4 us (10%)
  starting transfers between devices  57.4 us (7%)
  between operations  28.4 us (3%)
  other arithmetic  21.1 us (2%)
    unnamed x2, waiting for transfers between devices  221 us
    unnamed x1, blocking collectives  155 us
    dot_general x60, matrix products, dot(): return lax.dot_general(a, b, (dims, ((), ())), preferred_element_type=F32)  105 us
    psum x1, blocking collectives, local(): z_sum = lax.psum(z_part, ('x', 'z'))  70.3 us
    psum x1, blocking collectives, local(): density = lax.psum(jnp.stack(entries), OCC_AUX)  65.8 us
    ppermute x16, starting transfers between devices, down(): return lax.ppermute(v, axis, ring(4, -1))  45.5 us
    unnamed x108, local copies, waits for them, and re-layouts  43.6 us
    ppermute x16, waiting for transfers between devices, up(): return lax.ppermute(v, axis, ring(4, 1))  18.2 us
  transfers between devices with their start and end apart: 39, of which 10 were waited for; matrix products, arithmetic and copies ran while one was open for 22% of the time, Pallas kernels for 0%

profile of v1, /device:TPU:0, one launch (start us, length us, event | category | flops | bytes accessed | tf_op | source)
XLA Modules:
  0.0 838.7 jit_solution(4391718574668692102)
XLA Ops:
  28.6 13.4 %fusion.165 = (bf16[1,375,4000]{2,0,1:T(2,128)(2,1)}, bf16[1,375,4000]{2,0,1:T(2,128)(2,1)}) fusion(bf16[2,375,4000]{2,0,1:T(2,128)(2,1)} %param.14), kind=kLoop, calls=%fused_computation.334 | loop fusion | bytes 12000000 | tf_op jit(solution)/shard_map/slice | solution.py:112
  42.0 13.8 %copy.135 = bf16[1,375,4000]{1,2,0:T(8,128)(2,1)S(1)} copy(bf16[1,375,4000]{2,0,1:T(2,128)(2,1)} %get-tuple-element.35) | data formatting | bytes 6000000
  56.8 13.9 %copy.134 = bf16[1,375,4000]{1,2,0:T(8,128)(2,1)S(1)} copy(bf16[1,375,4000]{2,0,1:T(2,128)(2,1)} %get-tuple-element.34) | data formatting | bytes 6000000
  80.8 2.8 fusion.79
  83.6 2.8 fusion.81
  107.6 2.8 fusion.55
  112.0 2.8 fusion.51
  114.8 2.8 fusion.45
  120.3 2.8 fusion.49
  123.1 2.8 fusion.59
  128.7 2.7 fusion.57
  133.4 221.0 %all-reduce.4.cloned.1.call-done = f32[32,6,125]{2,1,0:T(8,128)} async-done(((f32[32,6,125]{2,1,0:T(8,128)}), f32[32,6,125]{2,1,0:T(8,128)}) %all-reduce.4.cloned.1.call-update) | async-done | bytes 96016
  356.4 154.6 %all-reduce.1 = f32[32,6,15]{2,1,0:T(8,128)S(1)} all-reduce(f32[32,6,15]{2,1,0:T(8,128)S(1)} %copy.133), channel_id=3, replica_groups=mesh['yh'=2,'core'=2,'x'=4,'z'=4,'yl'=2] {'x','z','yl'}, use_global_device_ids=true, to_apply=%region_10.11.clone | all-reduce | flops 2880 | bytes 23040
  520.2 3.2 collective-permute-start.5
  531.2 3.2 collective-permute-start.21
  537.8 70.3 %psum.14 = f32[2,4,1920]{2,1,0:T(4,128)S(1)} all-reduce(f32[2,4,1920]{2,1,0:T(4,128)S(1)} %pad_maximum_fusion.14), channel_id=1, replica_groups=mesh['yh'=2,'core'=2,'x'=4,'z'=4,'yl'=2] {'x','z'}, use_global_device_ids=true, to_apply=%region_0.1 | all-reduce | flops 15360 | bytes 122880 | tf_op jit(solution)/shard_map/psum | solution.py:138
  623.7 3.4 collective-permute-done.4
  629.2 3.2 collective-permute-start.9
  635.9 3.2 collective-permute-start.25
  639.3 3.7 collective-permute-start.10
  643.2 3.3 collective-permute-start.26
  647.1 3.5 collective-permute-done.24
  654.5 3.3 collective-permute-start.27
  668.3 65.8 %psum.15 = f32[3]{0:T(128)S(1)} all-reduce(f32[3]{0:T(128)S(1)} %pad_maximum_fusion.17), channel_id=1, replica_groups=mesh['yh'=2,'core'=2,'x'=4,'z'=4,'yl'=2] {'yh','core','x','z','yl'}, use_global_device_ids=true, to_apply=%region_17.18 | all-reduce | flops 3 | bytes 24 | tf_op jit(solution)/shard_map/psum | solution.py:174
  758.4 3.0 collective-permute-start.15
  761.3 3.1 fusion.43
  764.4 2.9 fusion.69
  768.5 6.9 collective-permute-done.32
  775.6 3.3 collective-permute-start.34
  782.7 3.2 collective-permute-start.18
  805.9 3.0 copy.121
  821.4 6.9 collective-permute-done.35
  (314 shorter events, 172.9 us)
Async XLA Ops:
  7.2 347.3 %all-reduce.4.cloned.1.call-start = ((), (), s32[]{:S(2)}) async-start(), calls=%async_computation | async-start | bytes 262144
  13.1 112.8 %collective-permute-start.1 = (bf16[375,1920]{1,0:T(8,128)(2,1)}, bf16[375,1920]{1,0:T(8,128)(2,1)}, u32[]{:S(2)}, u32[]{:S(2)}) collective-permute-start(bf16[375,1920]{1,0:T(8,128)(2,1)} %dynamic-slice_bitcast_fusion), channel_id=1, source_target_pairs={{0,1},{1,0},{32,97},{33,96},{64,65},{65,64},{96,33},{97,32},{2,3},... | collective-permute-start | bytes 4320008 | tf_op jit(solution)/shard_map/ppermute | solution.py:82
  26.0 485.6 %collective-permute-start = (bf16[1024,375]{0,1:T(8,128)(2,1)}, bf16[1024,375]{0,1:T(8,128)(2,1)}, u32[]{:S(2)}, u32[]{:S(2)}) collective-permute-start(bf16[1024,375]{0,1:T(8,128)(2,1)} %copy.104), channel_id=1, source_target_pairs={{0,1},{1,0},{32,97},{33,96},{64,65},{65,64},{96,33},{97,32},{2,3},... | collective-permute-start | bytes 2304008 | tf_op jit(solution)/shard_map/ppermute | solution.py:82
  26.4 510.8 %collective-permute-start.36 = (bf16[4,375]{1,0:T(4,128)(2,1)S(1)}, bf16[4,375]{1,0:T(4,128)(2,1)S(1)}, u32[]{:S(2)}, u32[]{:S(2)}) collective-permute-start(bf16[4,375]{1,0:T(4,128)(2,1)S(1)} %reshape.436), channel_id=1, source_target_pairs={{0,1},{1,0},{2,3},{3,2},{4,5},{5,4},{6,7},{7,6},{8,9},{9,8},{10,11... | collective-permute-start | bytes 9008 | tf_op jit(solution)/shard_map/ppermute | solution.py:131
  126.0 388.0 %collective-permute-start.2 = (bf16[375,1920]{1,0:T(8,128)(2,1)}, bf16[375,1920]{1,0:T(8,128)(2,1)}, u32[]{:S(2)}, u32[]{:S(2)}) collective-permute-start(bf16[375,1920]{1,0:T(8,128)(2,1)} %collective-permute-done.1), channel_id=1, source_target_pairs={{0,32},{32,0},{1,33},{33,1},{2,34},{34,2},{3,35},{35,3},{4,36},{36... | collective-permute-start | bytes 4320008 | tf_op jit(solution)/shard_map/ppermute | solution.py:85
  517.8 92.3 %collective-permute-start.3 = (bf16[128,1920]{1,0:T(8,128)(2,1)}, bf16[128,1920]{1,0:T(8,128)(2,1)}, u32[]{:S(2)}, u32[]{:S(2)}) collective-permute-start(bf16[128,1920]{1,0:T(8,128)(2,1)} %fusion.13), channel_id=1, source_target_pairs={{0,8},{8,16},{16,24},{24,0},{1,9},{9,17},{17,25},{25,1},{2,10},{10... | collective-permute-start | bytes 1474568 | tf_op jit(solution)/shard_map/ppermute | solution.py:22
  520.2 91.6 %collective-permute-start.5 = (bf16[128,1920]{1,0:T(8,128)(2,1)}, bf16[128,1920]{1,0:T(8,128)(2,1)}, u32[]{:S(2)}, u32[]{:S(2)}) collective-permute-start(bf16[128,1920]{1,0:T(8,128)(2,1)} %fusion.17), channel_id=1, source_target_pairs={{0,24},{8,0},{16,8},{24,16},{1,25},{9,1},{17,9},{25,17},{2,26},{10... | collective-permute-start | bytes 1474568 | tf_op jit(solution)/shard_map/ppermute | solution.py:26
  528.7 88.0 %collective-permute-start.19 = (bf16[128,1920]{1,0:T(8,128)(2,1)}, bf16[128,1920]{1,0:T(8,128)(2,1)}, u32[]{:S(2)}, u32[]{:S(2)}) collective-permute-start(bf16[128,1920]{1,0:T(8,128)(2,1)} %fusion.19), channel_id=1, source_target_pairs={{0,2},{2,4},{4,6},{6,0},{1,3},{3,5},{5,7},{7,1},{8,10},{10,12},{12... | collective-permute-start | bytes 1474568 | tf_op jit(solution)/shard_map/ppermute | solution.py:22
  531.2 87.5 %collective-permute-start.21 = (bf16[128,1920]{1,0:T(8,128)(2,1)}, bf16[128,1920]{1,0:T(8,128)(2,1)}, u32[]{:S(2)}, u32[]{:S(2)}) collective-permute-start(bf16[128,1920]{1,0:T(8,128)(2,1)} %fusion.23), channel_id=1, source_target_pairs={{0,6},{2,0},{4,2},{6,4},{1,7},{3,1},{5,3},{7,5},{8,14},{10,8},{12,... | collective-permute-start | bytes 1474568 | tf_op jit(solution)/shard_map/ppermute | solution.py:26
  611.7 15.4 %collective-permute-start.4 = (bf16[256,1920]{1,0:T(8,128)(2,1)S(1)}, bf16[256,1920]{1,0:T(8,128)(2,1)S(1)}, u32[]{:S(2)}, u32[]{:S(2)}) collective-permute-start(bf16[256,1920]{1,0:T(8,128)(2,1)S(1)} %pad_maximum_fusion.4), channel_id=1, source_target_pairs={{0,8},{8,16},{16,24},{24,0},{1,9},{9,17},{17,25},{25,1},{2,10},{10... | collective-permute-start | bytes 2949128 | tf_op jit(solution)/shard_map/ppermute | solution.py:22
  614.5 14.2 %collective-permute-start.6 = (bf16[256,1920]{1,0:T(8,128)(2,1)S(1)}, bf16[256,1920]{1,0:T(8,128)(2,1)S(1)}, u32[]{:S(2)}, u32[]{:S(2)}) collective-permute-start(bf16[256,1920]{1,0:T(8,128)(2,1)S(1)} %pad_maximum_fusion.5), channel_id=1, source_target_pairs={{0,24},{8,0},{16,8},{24,16},{1,25},{9,1},{17,9},{25,17},{2,26},{10... | collective-permute-start | bytes 2949128 | tf_op jit(solution)/shard_map/ppermute | solution.py:26
  618.4 15.6 %collective-permute-start.20 = (bf16[256,1920]{1,0:T(8,128)(2,1)S(1)}, bf16[256,1920]{1,0:T(8,128)(2,1)S(1)}, u32[]{:S(2)}, u32[]{:S(2)}) collective-permute-start(bf16[256,1920]{1,0:T(8,128)(2,1)S(1)} %pad_maximum_fusion.6), channel_id=1, source_target_pairs={{0,2},{2,4},{4,6},{6,0},{1,3},{3,5},{5,7},{7,1},{8,10},{10,12},{12... | collective-permute-start | bytes 2949128 | tf_op jit(solution)/shard_map/ppermute | solution.py:22
  621.2 14.2 %collective-permute-start.22 = (bf16[256,1920]{1,0:T(8,128)(2,1)S(1)}, bf16[256,1920]{1,0:T(8,128)(2,1)S(1)}, u32[]{:S(2)}, u32[]{:S(2)}) collective-permute-start(bf16[256,1920]{1,0:T(8,128)(2,1)S(1)} %pad_maximum_fusion.7), channel_id=1, source_target_pairs={{0,6},{2,0},{4,2},{6,4},{1,7},{3,1},{5,3},{7,5},{8,14},{10,8},{12,... | collective-permute-start | bytes 2949128 | tf_op jit(solution)/shard_map/ppermute | solution.py:26
  629.1 10.0 %collective-permute-start.7 = (bf16[32,1920]{1,0:T(8,128)(2,1)S(1)}, bf16[32,1920]{1,0:T(8,128)(2,1)S(1)}, u32[]{:S(2)}, u32[]{:S(2)}) collective-permute-start(bf16[32,1920]{1,0:T(8,128)(2,1)S(1)} %get-tuple-element.50), channel_id=1, source_target_pairs={{0,2},{2,4},{4,6},{6,0},{1,3},{3,5},{5,7},{7,1},{8,10},{10,12},{12... | collective-permute-start | bytes 368648 | tf_op jit(solution)/shard_map/ppermute | solution.py:22
  654.5 83.2 %collective-permute-start.27 = (bf16[64,1920]{1,0:T(8,128)(2,1)}, bf16[64,1920]{1,0:T(8,128)(2,1)}, u32[]{:S(2)}, u32[]{:S(2)}) collective-permute-start(bf16[64,1920]{1,0:T(8,128)(2,1)} %get-tuple-element.30), channel_id=1, source_target_pairs={{0,24},{8,0},{16,8},{24,16},{1,25},{9,1},{17,9},{25,17},{2,26},{10... | collective-permute-start | bytes 737288 | tf_op jit(solution)/shard_map/ppermute | solution.py:26
  657.8 77.0 %collective-permute-start.28 = (bf16[64,1920]{1,0:T(8,128)(2,1)}, bf16[64,1920]{1,0:T(8,128)(2,1)}, u32[]{:S(2)}, u32[]{:S(2)}) collective-permute-start(bf16[64,1920]{1,0:T(8,128)(2,1)} %get-tuple-element.30), channel_id=1, source_target_pairs={{0,8},{8,16},{16,24},{24,0},{1,9},{9,17},{17,25},{25,1},{2,10},{10... | collective-permute-start | bytes 737288 | tf_op jit(solution)/shard_map/ppermute | solution.py:22
  658.5 84.3 %collective-permute-start.11 = (bf16[64,1920]{1,0:T(8,128)(2,1)S(1)}, bf16[64,1920]{1,0:T(8,128)(2,1)}, u32[]{:S(2)}, u32[]{:S(2)}) collective-permute-start(bf16[64,1920]{1,0:T(8,128)(2,1)S(1)} %get-tuple-element.58), channel_id=1, source_target_pairs={{0,6},{2,0},{4,2},{6,4},{1,7},{3,1},{5,3},{7,5},{8,14},{10,8},{12,... | collective-permute-start | bytes 737288 | tf_op jit(solution)/shard_map/ppermute | solution.py:26
  661.1 78.9 %collective-permute-start.12 = (bf16[64,1920]{1,0:T(8,128)(2,1)S(1)}, bf16[64,1920]{1,0:T(8,128)(2,1)}, u32[]{:S(2)}, u32[]{:S(2)}) collective-permute-start(bf16[64,1920]{1,0:T(8,128)(2,1)S(1)} %get-tuple-element.58), channel_id=1, source_target_pairs={{0,2},{2,4},{4,6},{6,0},{1,3},{3,5},{5,7},{7,1},{8,10},{10,12},{12... | collective-permute-start | bytes 737288 | tf_op jit(solution)/shard_map/ppermute | solution.py:22
  668.2 65.9 %collective-permute-start.37 = (f32[2,15]{1,0:T(2,128)S(1)}, f32[2,15]{1,0:T(2,128)S(1)}, u32[]{:S(2)}, u32[]{:S(2)}) collective-permute-start(f32[2,15]{1,0:T(2,128)S(1)} %constant_dynamic-slice_fusion), channel_id=1, source_target_pairs={{0,1},{1,0},{2,3},{3,2},{4,5},{5,4},{6,7},{7,6},{8,9},{9,8},{10,11... | collective-permute-start | bytes 368 | tf_op jit(solution)/shard_map/ppermute | solution.py:185
  735.7 12.8 %collective-permute-start.29 = (bf16[32,1920]{1,0:T(8,128)(2,1)S(1)}, bf16[32,1920]{1,0:T(8,128)(2,1)S(1)}, u32[]{:S(2)}, u32[]{:S(2)}) collective-permute-start(bf16[32,1920]{1,0:T(8,128)(2,1)S(1)} %slice.420), channel_id=1, source_target_pairs={{0,8},{8,16},{16,24},{24,0},{1,9},{9,17},{17,25},{25,1},{2,10},{10... | collective-permute-start | bytes 368648 | tf_op jit(solution)/shard_map/ppermute | solution.py:22
  738.6 10.6 %collective-permute-start.30 = (bf16[32,1920]{1,0:T(8,128)(2,1)S(1)}, bf16[32,1920]{1,0:T(8,128)(2,1)S(1)}, u32[]{:S(2)}, u32[]{:S(2)}) collective-permute-start(bf16[32,1920]{1,0:T(8,128)(2,1)S(1)} %slice.421), channel_id=1, source_target_pairs={{0,24},{8,0},{16,8},{24,16},{1,25},{9,1},{17,9},{25,17},{2,26},{10... | collective-permute-start | bytes 368648 | tf_op jit(solution)/shard_map/ppermute | solution.py:26
  740.9 13.8 %collective-permute-start.13 = (bf16[32,1920]{1,0:T(8,128)(2,1)S(1)}, bf16[32,1920]{1,0:T(8,128)(2,1)S(1)}, u32[]{:S(2)}, u32[]{:S(2)}) collective-permute-start(bf16[32,1920]{1,0:T(8,128)(2,1)S(1)} %slice.392), channel_id=1, source_target_pairs={{0,2},{2,4},{4,6},{6,0},{1,3},{3,5},{5,7},{7,1},{8,10},{10,12},{12... | collective-permute-start | bytes 368648 | tf_op jit(solution)/shard_map/ppermute | solution.py:22
  743.8 11.6 %collective-permute-start.14 = (bf16[32,1920]{1,0:T(8,128)(2,1)S(1)}, bf16[32,1920]{1,0:T(8,128)(2,1)S(1)}, u32[]{:S(2)}, u32[]{:S(2)}) collective-permute-start(bf16[32,1920]{1,0:T(8,128)(2,1)S(1)} %slice.393), channel_id=1, source_target_pairs={{0,6},{2,0},{4,2},{6,4},{1,7},{3,1},{5,3},{7,5},{8,14},{10,8},{12,... | collective-permute-start | bytes 368648 | tf_op jit(solution)/shard_map/ppermute | solution.py:26
  751.5 23.9 %collective-permute-start.32 = (bf16[256,1920]{1,0:T(8,128)(2,1)}, bf16[256,1920]{1,0:T(8,128)(2,1)S(1)}, u32[]{:S(2)}, u32[]{:S(2)}) collective-permute-start(bf16[256,1920]{1,0:T(8,128)(2,1)} %constant_dynamic-update-slice_fusion.7), channel_id=1, source_target_pairs={{0,2},{2,4},{4,6},{6,0},{1,3},{3,5},{5,7},{7,1},{8,10},{10,12},{12... | collective-permute-start | bytes 2949128 | tf_op jit(solution)/shard_map/ppermute | solution.py:22
  752.1 23.4 %collective-permute-start.31 = (bf16[256,1920]{1,0:T(8,128)(2,1)}, bf16[256,1920]{1,0:T(8,128)(2,1)S(1)}, u32[]{:S(2)}, u32[]{:S(2)}) collective-permute-start(bf16[256,1920]{1,0:T(8,128)(2,1)} %constant_dynamic-update-slice_fusion.7), channel_id=1, source_target_pairs={{0,6},{2,0},{4,2},{6,4},{1,7},{3,1},{5,3},{7,5},{8,14},{10,8},{12,... | collective-permute-start | bytes 2949128 | tf_op jit(solution)/shard_map/ppermute | solution.py:26
  757.7 23.4 %collective-permute-start.16 = (bf16[256,1920]{1,0:T(8,128)(2,1)}, bf16[256,1920]{1,0:T(8,128)(2,1)S(1)}, u32[]{:S(2)}, u32[]{:S(2)}) collective-permute-start(bf16[256,1920]{1,0:T(8,128)(2,1)} %constant_dynamic-update-slice_fusion), channel_id=1, source_target_pairs={{0,8},{8,16},{16,24},{24,0},{1,9},{9,17},{17,25},{25,1},{2,10},{10... | collective-permute-start | bytes 2949128 | tf_op jit(solution)/shard_map/ppermute | solution.py:22
  758.4 23.5 %collective-permute-start.15 = (bf16[256,1920]{1,0:T(8,128)(2,1)}, bf16[256,1920]{1,0:T(8,128)(2,1)S(1)}, u32[]{:S(2)}, u32[]{:S(2)}) collective-permute-start(bf16[256,1920]{1,0:T(8,128)(2,1)} %constant_dynamic-update-slice_fusion), channel_id=1, source_target_pairs={{0,24},{8,0},{16,8},{24,16},{1,25},{9,1},{17,9},{25,17},{2,26},{10... | collective-permute-start | bytes 2949128 | tf_op jit(solution)/shard_map/ppermute | solution.py:26
  775.5 20.0 %collective-permute-start.33 = (bf16[128,1920]{1,0:T(8,128)(2,1)S(1)}, bf16[128,1920]{1,0:T(8,128)(2,1)S(1)}, u32[]{:S(2)}, u32[]{:S(2)}) collective-permute-start(bf16[128,1920]{1,0:T(8,128)(2,1)S(1)} %slice.422), channel_id=1, source_target_pairs={{0,2},{2,4},{4,6},{6,0},{1,3},{3,5},{5,7},{7,1},{8,10},{10,12},{12... | collective-permute-start | bytes 1474568 | tf_op jit(solution)/shard_map/ppermute | solution.py:22
  775.6 19.9 %collective-permute-start.34 = (bf16[128,1920]{1,0:T(8,128)(2,1)S(1)}, bf16[128,1920]{1,0:T(8,128)(2,1)S(1)}, u32[]{:S(2)}, u32[]{:S(2)}) collective-permute-start(bf16[128,1920]{1,0:T(8,128)(2,1)S(1)} %slice.423), channel_id=1, source_target_pairs={{0,6},{2,0},{4,2},{6,4},{1,7},{3,1},{5,3},{7,5},{8,14},{10,8},{12,... | collective-permute-start | bytes 1474568 | tf_op jit(solution)/shard_map/ppermute | solution.py:26
  781.9 18.4 %collective-permute-start.17 = (bf16[128,1920]{1,0:T(8,128)(2,1)}, bf16[128,1920]{1,0:T(8,128)(2,1)}, u32[]{:S(2)}, u32[]{:S(2)}) collective-permute-start(bf16[128,1920]{1,0:T(8,128)(2,1)} %slice.394), channel_id=1, source_target_pairs={{0,8},{8,16},{16,24},{24,0},{1,9},{9,17},{17,25},{25,1},{2,10},{10... | collective-permute-start | bytes 1474568 | tf_op jit(solution)/shard_map/ppermute | solution.py:22
  782.7 18.7 %collective-permute-start.18 = (bf16[128,1920]{1,0:T(8,128)(2,1)}, bf16[128,1920]{1,0:T(8,128)(2,1)}, u32[]{:S(2)}, u32[]{:S(2)}) collective-permute-start(bf16[128,1920]{1,0:T(8,128)(2,1)} %slice.395), channel_id=1, source_target_pairs={{0,24},{8,0},{16,8},{24,16},{1,25},{9,1},{17,9},{25,17},{2,26},{10... | collective-permute-start | bytes 1474568 | tf_op jit(solution)/shard_map/ppermute | solution.py:26
  811.5 16.7 %collective-permute-start.35 = (bf16[4,4,64,375]{3,2,1,0:T(8,128)(2,1)}, bf16[4,4,64,375]{3,2,1,0:T(8,128)(2,1)}, u32[]{:S(2)}, u32[]{:S(2)}) collective-permute-start(bf16[4,4,64,375]{3,2,1,0:T(8,128)(2,1)} %fusion.32), channel_id=1, source_target_pairs={{0,1},{1,0},{2,3},{3,2},{4,5},{5,4},{6,7},{7,6},{8,9},{9,8},{10,11... | collective-permute-start | bytes 2304008 | tf_op jit(solution)/shard_map/ppermute | solution.py:199
  (55 other events, 266.6 us)
Sparse Core Ops, SparseCore 0:
  73.5 280.9 all-reduce.3
